TPU v7x, 512 devices: a whole 4x8x8 slice. The times are simulated.
512 devices in a mesh: src: 16 (over z, core), tm: 32 (over x, y).
Axes of the slice: x: 4, y: 8, z: 8, core: 2. Of those that a mesh axis runs over, the one named last changes fastest.
Arguments:
- greens: bfloat16 [65536, 12288], P('tm', 'src')
- pairs: int32 [16, 2], P('src'), may hold values from 0 to 15, as said below
- onsets: int32 [16], replicated, may hold values from 0 to 32767
Outputs:
- gram: float32 [16, 768, 768], P('src', 'tm')
Inputs may be any that keep to these rules, and one draw needn't show every extreme that they name: `pairs`: row s names the blocks s and (s - 1) mod 16, in either order.
All inputs are finite; a program needn't handle non-finite values.
Results may differ from a plain program's by a relative error of at most 0.0003.
Values may be sent and summed in bfloat16 or wider, within the bound.
A program may use at most 64 MiB of HBM per device.

v0:
```python
import jax
import jax.numpy as jnp
from jax import lax
from jax.sharding import Mesh
from jax.sharding import PartitionSpec as P

TM = ("tm_0", "tm_1")


def from_behind(value, axis, by):
    length = lax.axis_size(axis)
    return lax.ppermute(value, axis, [(i, (i + by) % length) for i in range(length)])


def over_axes(value, axes):
    for axis in axes:
        value = lax.psum(value, axis)
    return value


def cut_along(value, dim, length):
    lengths = value.shape
    tiles = value.reshape(*lengths[:dim], length, lengths[dim] // length, *lengths[dim + 1 :])
    return jnp.moveaxis(tiles, dim, 0)


def sent_and_summed(value, axis, dim):
    length = lax.axis_size(axis)
    tiles = lax.all_to_all(cut_along(value, dim, length), axis, 0, 0, tiled=True)
    return jnp.sum(tiles, axis=0)


def on_device(greens, pairs, onsets):
    rows_dev, width = greens.shape
    row_group = lax.axis_index(TM)
    row_start = row_group * rows_dev
    owner = lax.axis_index("src")
    lower = from_behind(greens, "src", 1)
    first = pairs[0, 0]
    second = pairs[0, 1]
    row_ids = row_start + jnp.arange(rows_dev, dtype=jnp.int32)
    left = jnp.where(first == owner, greens, lower)
    right = jnp.where(first == owner, lower, greens)
    left = jnp.where((row_ids >= onsets[first])[:, None], left, jnp.zeros_like(left))
    right = jnp.where((row_ids >= onsets[second])[:, None], right, jnp.zeros_like(right))
    left_f = left.astype(jnp.float32)
    right_f = right.astype(jnp.float32)
    norm_left, norm_right = (
        over_axes(jnp.sum(left_f * left_f, axis=0), TM),
        over_axes(jnp.sum(right_f * right_f, axis=0), TM),
    )
    arrival = jnp.maximum(onsets[first], onsets[second])
    silent = row_start + rows_dev <= arrival
    share = width // lax.axis_size(TM)
    piece = left
    mine = sent_and_summed(
        lax.cond(
            silent,
            lambda: jnp.zeros((share * lax.axis_size(TM), width), jnp.float32),
            lambda: lax.dot_general(
                piece, right, (((0,), (0,)), ((), ())), preferred_element_type=jnp.float32
            ),
        ),
        TM,
        0,
    )
    scale_rows = lax.dynamic_slice_in_dim(lax.rsqrt(norm_left + 1e-06), row_group * share, share, 0)
    scale_cols = lax.rsqrt(norm_right + 1e-06)
    normalized = mine * scale_rows[:, None] * scale_cols[None, :]
    return normalized[None]


def solution(mesh):
    split = Mesh(mesh.devices.reshape(mesh.shape["src"], 4, 8), ("src", "tm_0", "tm_1"))
    in_specs = (P(TM, "src"), P("src", None), P())
    out_specs = P("src", TM, None)
    return jax.shard_map(
        on_device, mesh=split, in_specs=in_specs, out_specs=out_specs, check_vma=False
    )
```

profile of v0, /device:TPU:194, one launch (start us, length us, event | category | flops | bytes accessed | tf_op | source)
XLA Modules:
  0.0 122.4 jit_solution(4111299855507646524)
XLA Ops:
  0.0 0.0 collective-permute-start
  0.0 1.3 %fusion.4 = (s32[1,1]{1,0:T(1,128)}, s32[1,1]{1,0:T(1,128)}) fusion(s32[1,2]{1,0:T(1,128)} %param.6), kind=kLoop, calls=%fused_computation.12 | loop fusion | bytes 16 | tf_op jit(solution)/shard_map/slice | solution.py:40
  6.0 1.4 %fusion.3 = (s32[1]{0:T(128)}, s32[1]{0:T(128)}) fusion(s32[16]{0:T(128)} %param.7, s32[]{:T(128)S(6)} %select_n.31, s32[]{:T(128)S(6)} %select_n.30), kind=kLoop, calls=%fused_computation.11 | loop fusion | bytes 24 | tf_op jit(solution)/shard_map/dynamic_slice | solution.py:52
  8.8 1.3 %fusion.1 = (pred[2048]{0:T(1024)(128)(4,1)S(1)}, pred[2048]{0:T(1024)(128)(4,1)S(1)}) fusion(s32[]{:T(128)} %bitcast.3, s32[]{:T(128)S(6)} %mul.46, s32[]{:T(128)} %bitcast.1), kind=kLoop, calls=%fused_computation.7 | loop fusion | flops 6144 | bytes 4108 | tf_op jit(solution)/shard_map/ge | solution.py:45
  10.1 26.8 %collective-permute-done = bf16[2048,768]{1,0:T(8,128)(2,1)S(1)} collective-permute-done((bf16[2048,768]{1,0:T(8,128)(2,1)}, bf16[2048,768]{1,0:T(8,128)(2,1)S(1)}, u32[]{:S(2)}, u32[]{:S(2)}) %collective-permute-start) | collective-permute-done | bytes 3145760 | tf_op jit(solution)/shard_map/ppermute | solution.py:12
  36.9 4.6 %multiply_reduce_fusion = (f32[768]{0:T(1024)S(1)}, bf16[2048,768]{1,0:T(8,128)(2,1)S(1)}, f32[768]{0:T(1024)S(1)}, bf16[2048,768]{1,0:T(8,128)(2,1)S(1)}) fusion(bf16[2048,768]{1,0:T(8,128)(2,1)S(1)} %collective-permute-done, bf16[2048,768]{1,0:T(8,128)(2,1)} %param.5, pred[]{:T(512)S(6)} %eq.4, pred[2048]{0:T(1024)(128)(4,1)S(1)} %get-tuple-element.28, ...), kind=kLoop, calls=%fused_computation | loop fusion | flops 15727104 | bytes 12593153 | tf_op jit(solution)/shard_map/reduce_sum | solution.py:50
  41.5 0.2 conditional.1
  41.6 0.2 broadcast.59
  41.7 0.0 copy-start
  41.7 1.4 %copy-done = f32[768,768]{1,0:T(8,128)} copy-done((f32[768,768]{1,0:T(8,128)}, f32[768,768]{1,0:T(8,128)S(1)}, u32[]{:S(2)}) %copy-start) | copy-done | bytes 2359320
  43.1 12.9 %all-to-all-start = ((f32[32,24,768]{2,1,0:T(8,128)}), f32[32,24,768]{2,1,0:T(8,128)S(1)}, u32[]{:S(2)}, u32[]{:S(2)}) async-start(f32[32,24,768]{2,1,0:T(8,128)} %bitcast.11), calls=%async_computation | async-start | bytes 4718592 | tf_op jit(solution)/shard_map/all_to_all | solution.py:29
  56.0 9.5 %all-reduce.1 = (f32[768]{0:T(1024)S(1)}, f32[768]{0:T(1024)S(1)}) all-reduce(f32[768]{0:T(1024)S(1)} %get-tuple-element.20, f32[768]{0:T(1024)S(1)} %get-tuple-element.22), channel_id=1, replica_groups=mesh['src'=16,'tm_0'=4,'tm_1'=8] {'tm_0'}, use_global_device_ids=true, to_apply=%region_7.8 | all-reduce | flops 1536 | bytes 12288 | tf_op jit(solution)/shard_map/psum | solution.py:17
  65.5 56.0 %all-reduce = (f32[768]{0:T(1024)S(1)}, f32[768]{0:T(1024)S(1)}) all-reduce(f32[768]{0:T(1024)S(1)} %get-tuple-element.16, f32[768]{0:T(1024)S(1)} %get-tuple-element.17), channel_id=1, replica_groups=mesh['src'=16,'tm_0'=4,'tm_1'=8] {'tm_1'}, use_global_device_ids=true, to_apply=%region_8.9 | all-reduce | flops 1536 | bytes 12288 | tf_op jit(solution)/shard_map/psum | solution.py:17
  121.5 0.1 dynamic_slice.13
  121.6 0.0 all-to-all-done
  121.6 0.1 reduce_sum.29
  121.7 0.7 fusion
  (2 shorter events, 0.0 us)
Async XLA Ops:
  0.0 36.9 %collective-permute-start = (bf16[2048,768]{1,0:T(8,128)(2,1)}, bf16[2048,768]{1,0:T(8,128)(2,1)S(1)}, u32[]{:S(2)}, u32[]{:S(2)}) collective-permute-start(bf16[2048,768]{1,0:T(8,128)(2,1)} %param.5), channel_id=1, source_target_pairs={{0,32},{32,64},{64,96},{96,128},{128,160},{160,192},{192,224},{224... | collective-permute-start | bytes 9437192 | tf_op jit(solution)/shard_map/ppermute | solution.py:12
  41.7 1.4 %copy-start = (f32[768,768]{1,0:T(8,128)}, f32[768,768]{1,0:T(8,128)S(1)}, u32[]{:S(2)}) copy-start(f32[768,768]{1,0:T(8,128)S(1)} %get-tuple-element.30) | copy-start | bytes 7077892
  43.1 78.5 %all-to-all-start = ((f32[32,24,768]{2,1,0:T(8,128)}), f32[32,24,768]{2,1,0:T(8,128)S(1)}, u32[]{:S(2)}, u32[]{:S(2)}) async-start(f32[32,24,768]{2,1,0:T(8,128)} %bitcast.11), calls=%async_computation | async-start | bytes 4718592 | tf_op jit(solution)/shard_map/all_to_all | solution.py:29
where the time goes:
time: 123 us; the launch traced here: 122 us
  blocking collectives  65.5 us (53%)
  waiting for transfers between devices  26.8 us (22%)
  starting transfers between devices  12.9 us (10%)
  other arithmetic  6.8 us (6%)
  between operations  6.13 us (5%)
  local copies, waits for them, and re-layouts  4.37 us (4%)
    psum x2, blocking collectives, over_axes(): value = lax.psum(value, axis)  65.5 us
    ppermute x1, waiting for transfers between devices, from_behind(): lax.ppermute(value, axis, [(i, (i + by) % length) for i in range(length)])  26.8 us
    all_to_all x1, starting transfers between devices, sent_and_summed(): lax.all_to_all(cut_along(value, dim, length), axis, 0, 0, tiled=True)  12.9 us
    reduce_sum x1, other arithmetic, on_device(): jnp.sum(right_f * right_f, axis=0)  4.62 us
  transfers between devices with their start and end apart: 2, of which 1 were waited for; matrix products, arithmetic and copies ran while one was open for 3% of the time, Pallas kernels for 0%

commit v1 on v0

--- a/solution.py
+++ b/solution.py
@@ -14,7 +14,7 @@
 
 def over_axes(value, axes):
     for axis in axes:
-        value = lax.psum(value, axis)
+        value = jnp.sum(lax.all_gather(value, axis), axis=0)
     return value
 
 

time: 123 us -> 156 us (1.27)
  the two profiles are of different devices: /device:TPU:194 before, /device:TPU:192 now
where the time goes in v1:
time: 156 us; the launch traced here: 155 us
  blocking collectives  98.5 us (63%)
  waiting for transfers between devices  26.8 us (17%)
  starting transfers between devices  12.6 us (8%)
  other arithmetic  6.9 us (4%)
  between operations  6.16 us (4%)
  local copies, waits for them, and re-layouts  4.38 us (3%)
    all_gather x4, blocking collectives, over_axes(): value = jnp.sum(lax.all_gather(value, axis), axis=0)  98.5 us
    ppermute x1, waiting for transfers between devices, from_behind(): lax.ppermute(value, axis, [(i, (i + by) % length) for i in range(length)])  26.8 us
    all_to_all x1, starting transfers between devices, sent_and_summed(): lax.all_to_all(cut_along(value, dim, length), axis, 0, 0, tiled=True)  12.6 us
    reduce_sum x1, other arithmetic, on_device(): jnp.sum(right_f * right_f, axis=0)  4.62 us
  transfers between devices with their start and end apart: 2, of which 1 were waited for; matrix products, arithmetic and copies ran while one was open for 3% of the time, Pallas kernels for 0%

profile of v1, /device:TPU:192, one launch (start us, length us, event | category | flops | bytes accessed | tf_op | source)
XLA Modules:
  0.0 155.3 jit_solution(5253012441269563766)
XLA Ops:
  0.0 0.0 collective-permute-start
  0.0 1.3 fusion.4
  6.0 1.4 fusion.3
  8.8 1.3 fusion.1
  10.1 26.8 %collective-permute-done = bf16[2048,768]{1,0:T(8,128)(2,1)S(1)} collective-permute-done((bf16[2048,768]{1,0:T(8,128)(2,1)}, bf16[2048,768]{1,0:T(8,128)(2,1)S(1)}, u32[]{:S(2)}, u32[]{:S(2)}) %collective-permute-start) | collective-permute-done | bytes 3145760 | tf_op jit(solution)/shard_map/ppermute | solution.py:12
  36.9 4.6 %multiply_reduce_fusion = (f32[768]{0:T(1024)S(1)}, bf16[2048,768]{1,0:T(8,128)(2,1)S(1)}, f32[768]{0:T(1024)S(1)}, bf16[2048,768]{1,0:T(8,128)(2,1)S(1)}) fusion(bf16[2048,768]{1,0:T(8,128)(2,1)S(1)} %collective-permute-done, bf16[2048,768]{1,0:T(8,128)(2,1)} %param.5, pred[]{:T(512)S(6)} %eq.4, pred[2048]{0:T(1024)(128)(4,1)S(1)} %get-tuple-element.24, ...), kind=kLoop, calls=%fused_computation | loop fusion | flops 15727104 | bytes 12593153 | tf_op jit(solution)/shard_map/reduce_sum | solution.py:50
  41.5 0.2 conditional.1
  41.6 0.2 broadcast.62
  41.7 0.0 copy-start
  41.7 1.4 copy-done
  43.1 12.6 %all-to-all-start = ((f32[32,24,768]{2,1,0:T(8,128)}), f32[32,24,768]{2,1,0:T(8,128)S(1)}, u32[]{:S(2)}, u32[]{:S(2)}) async-start(f32[32,24,768]{2,1,0:T(8,128)} %bitcast.11), calls=%async_computation | async-start | bytes 4718592 | tf_op jit(solution)/shard_map/all_to_all | solution.py:29
  55.7 13.2 %all-gather.4 = f32[4,1,768]{2,1,0:T(1,128)S(1)} all-gather(f32[1,1,768]{2,1,0:T(1,128)S(1)} %reshape.69), channel_id=2, replica_groups=mesh['src'=16,'tm_0'=4,'tm_1'=8] {'tm_0'}, dimensions={0}, use_global_device_ids=true | all-gather | bytes 15360 | tf_op jit(solution)/shard_map/all_gather | solution.py:17
  69.0 11.9 %all-gather.6 = f32[4,1,768]{2,1,0:T(1,128)S(1)} all-gather(f32[1,1,768]{2,1,0:T(1,128)S(1)} %reshape.73), channel_id=4, replica_groups=mesh['src'=16,'tm_0'=4,'tm_1'=8] {'tm_0'}, dimensions={0}, use_global_device_ids=true | all-gather | bytes 15360 | tf_op jit(solution)/shard_map/all_gather | solution.py:17
  80.9 49.1 %all-gather.7 = f32[8,1,768]{2,1,0:T(1,128)S(1)} all-gather(f32[1,1,768]{2,1,0:T(1,128)S(1)} %reshape.75), channel_id=5, replica_groups=mesh['src'=16,'tm_0'=4,'tm_1'=8] {'tm_1'}, dimensions={0}, use_global_device_ids=true | all-gather | bytes 27648 | tf_op jit(solution)/shard_map/all_gather | solution.py:17
  130.0 24.4 %all-gather.5 = f32[8,1,768]{2,1,0:T(1,128)S(1)} all-gather(f32[1,1,768]{2,1,0:T(1,128)S(1)} %reshape.71), channel_id=3, replica_groups=mesh['src'=16,'tm_0'=4,'tm_1'=8] {'tm_1'}, dimensions={0}, use_global_device_ids=true | all-gather | bytes 27648 | tf_op jit(solution)/shard_map/all_gather | solution.py:17
  154.4 0.1 dynamic_slice.13
  154.5 0.0 all-to-all-done
  154.5 0.1 reduce_sum.65
  154.6 0.7 fusion
  (10 shorter events, 0.1 us)
Async XLA Ops:
  0.0 36.9 %collective-permute-start = (bf16[2048,768]{1,0:T(8,128)(2,1)}, bf16[2048,768]{1,0:T(8,128)(2,1)S(1)}, u32[]{:S(2)}, u32[]{:S(2)}) collective-permute-start(bf16[2048,768]{1,0:T(8,128)(2,1)} %param.5), channel_id=1, source_target_pairs={{0,32},{32,64},{64,96},{96,128},{128,160},{160,192},{192,224},{224... | collective-permute-start | bytes 9437192 | tf_op jit(solution)/shard_map/ppermute | solution.py:12
  41.7 1.4 copy-start
  43.1 111.3 %all-to-all-start = ((f32[32,24,768]{2,1,0:T(8,128)}), f32[32,24,768]{2,1,0:T(8,128)S(1)}, u32[]{:S(2)}, u32[]{:S(2)}) async-start(f32[32,24,768]{2,1,0:T(8,128)} %bitcast.11), calls=%async_computation | async-start | bytes 4718592 | tf_op jit(solution)/shard_map/all_to_all | solution.py:29
